TPU v7x, 32 devices: a whole 2x2x4 slice. The times are simulated.
32 devices in a mesh: chan: 16 (over z, x, core), rows: 2 (over y).
Axes of the slice: x: 2, y: 2, z: 4, core: 2. Of those that a mesh axis runs over, the one named last changes fastest.
Arguments:
- inputs: bfloat16 [1, 2, 256, 2048], P(None, 'rows', None, 'chan'), may hold values from -6 to 6
- weights: bfloat16 [3, 3, 2048, 2048], P(None, None, 'chan'), may hold values from -0.0625 to 0.0625
- cotangent: bfloat16 [1, 2, 256, 2048], P(None, 'rows', None, 'chan'), may hold values from -6 to 6
Outputs:
- outputs: bfloat16 [1, 2, 256, 2048], P(None, 'rows', None, 'chan')
- input_grad: bfloat16 [1, 2, 256, 2048], P(None, 'rows', None, 'chan')
- weight_grad: float32 [3, 3, 2048, 2048], P(None, None, 'chan', 'rows')
All inputs are finite; a program needn't handle non-finite values.
Results may differ from a plain program's by a relative error of at most 0.001.
Values may be sent and summed in bfloat16 or wider, within the bound.
A program may use at most 128 MiB of HBM per device.

v0:
```python
import jax
import jax.numpy as jnp
from jax import lax
from jax.sharding import PartitionSpec as P


def with_halo(array, sides, width):
    for axis, dim in sides:
        devices, length = (lax.axis_size(axis), array.shape[dim])
        up = [(i, (i + 1) % devices) for i in range(devices - 1)]
        down = [(j, i) for i, j in up]
        last = lax.slice_in_dim(array, length - width, length, axis=dim)
        initial = lax.slice_in_dim(array, 0, width, axis=dim)
        before = lax.ppermute(last, axis, up)
        after = lax.ppermute(initial, axis, down)
        array = jnp.concatenate([before, array, after], axis=dim)
    return array


def unfold(padded, height, breadth):
    taps = [
        padded[:, row_off : row_off + height, col_off : col_off + breadth, :]
        for row_off in range(3)
        for col_off in range(3)
    ]
    stacked = jnp.concatenate(taps, axis=3)
    return stacked.reshape(-1, stacked.shape[3])


def pad_columns(rimmed):
    return jnp.pad(rimmed, ((0, 0), (0, 0), (1, 1), (0, 0)))


def on_device(inputs, weights, cotangent):
    batches = inputs.shape[0]
    height = inputs.shape[1]
    breadth = inputs.shape[2]
    local_ch = inputs.shape[3]
    channels = weights.shape[3]
    pixels = batches * height * breadth
    contract_first = (((0,), (1,)), ((), ()))
    rimmed = with_halo(inputs, (("rows", 1),), 1)
    columns = unfold(pad_columns(rimmed), height, breadth)
    matrix = weights.reshape(9 * local_ch, channels)
    block = matrix
    conv_out = lax.psum_scatter(
        lax.dot_general(block, columns, contract_first, preferred_element_type=jnp.float32),
        "chan",
        scatter_dimension=0,
        tiled=True,
    )
    outputs = conv_out.T.reshape(batches, height, breadth, local_ch).astype(jnp.bfloat16)
    grad_rimmed = with_halo(cotangent, (("rows", 1),), 1)
    flipped = jnp.transpose(weights[::-1, ::-1], (2, 0, 1, 3))
    piece = lax.all_gather(grad_rimmed, "chan", axis=3, tiled=True)
    count = piece.shape[3]
    grad_cols = unfold(pad_columns(piece), height, breadth)
    block = flipped.reshape(local_ch, 9 * count)
    data_sum = lax.dot_general(
        block, grad_cols, (((1,), (1,)), ((), ())), preferred_element_type=jnp.float32
    )
    inner = piece[:, 1 : height + 1].reshape(pixels, count)
    update = lax.dot_general(
        columns, inner, (((0,), (0,)), ((), ())), preferred_element_type=jnp.float32
    )
    filter_sum = update
    data_sum, filter_sum = (data_sum, filter_sum)
    input_grad = data_sum.T.reshape(batches, height, breadth, local_ch).astype(jnp.bfloat16)
    total_pixels = pixels * lax.axis_size("rows")
    scaled = (filter_sum / jnp.sqrt(jnp.float32(total_pixels))).reshape(3, 3, local_ch, channels)
    weight_grad = lax.psum_scatter(scaled, "rows", scatter_dimension=3, tiled=True)
    return (outputs, input_grad, weight_grad)


def solution(mesh):
    in_specs = (
        P(None, "rows", None, "chan"),
        P(None, None, "chan", None),
        P(None, "rows", None, "chan"),
    )
    out_specs = (
        P(None, "rows", None, "chan"),
        P(None, "rows", None, "chan"),
        P(None, None, "chan", "rows"),
    )
    return jax.shard_map(
        on_device, mesh=mesh, in_specs=in_specs, out_specs=out_specs, check_vma=False
    )
```

profile of v0, /device:TPU:0, one launch (start us, length us, event | category | flops | bytes accessed | tf_op | source)
XLA Modules:
  0.0 250.3 jit_solution(17633905704568887612)
XLA Ops:
  7.2 0.0 all-gather.2.cloned.1.call-start
  7.2 4.9 %collective-permute-start.2 = (bf16[1,1,256,128]{3,2,1,0:T(8,128)(2,1)}, bf16[1,1,256,128]{3,2,1,0:T(8,128)(2,1)S(1)}, u32[]{:S(2)}, u32[]{:S(2)}) collective-permute-start(bf16[1,1,256,128]{3,2,1,0:T(8,128)(2,1)} %param.5), channel_id=1, source_target_pairs={{0,1},{2,3},{4,5},{6,7},{8,9},{10,11},{12,13},{14,15},{16,17},{18,... | collective-permute-start | bytes 196616 | tf_op jit(solution)/shard_map/ppermute | solution.py:14
  12.1 1.3 collective-permute-start.3
  13.4 0.9 collective-permute-done.2
  14.3 4.2 %collective-permute-done.3 = bf16[1,1,256,128]{3,2,1,0:T(8,128)(2,1)S(1)} collective-permute-done((bf16[1,1,256,128]{3,2,1,0:T(8,128)(2,1)}, bf16[1,1,256,128]{3,2,1,0:T(8,128)(2,1)S(1)}, u32[]{:S(2)}, u32[]{:S(2)}) %collective-permute-start.3) | collective-permute-done | bytes 65568 | tf_op jit(solution)/shard_map/ppermute | solution.py:15
  18.5 1.5 pad_maximum_fusion
  20.0 0.0 all-gather.2.cloned.1.call-update
  20.0 0.0 reduce-scatter.3.cloned.1.call-start
  20.1 1.7 collective-permute-start
  21.8 1.3 collective-permute-start.1
  23.1 0.9 collective-permute-done
  24.0 4.2 %collective-permute-done.1 = bf16[1,1,256,128]{3,2,1,0:T(8,128)(2,1)S(1)} collective-permute-done((bf16[1,1,256,128]{3,2,1,0:T(8,128)(2,1)}, bf16[1,1,256,128]{3,2,1,0:T(8,128)(2,1)S(1)}, u32[]{:S(2)}, u32[]{:S(2)}) %collective-permute-start.1) | collective-permute-done | bytes 65568 | tf_op jit(solution)/shard_map/ppermute | solution.py:15
  28.1 0.9 fusion.23
  29.1 0.9 constant_dynamic-update-slice_fusion.1
  30.1 5.2 %convolution_bitcast_fusion = f32[2048,256]{0,1:T(8,128)} fusion(bf16[1152,2048]{1,0:T(8,128)(2,1)} %bitcast.34, bf16[1,1,256,1152]{3,2,1,0:T(8,128)(2,1)S(1)} %slice_dynamic-update-slice_fusion.3), kind=kOutput, calls=%fused_computation.3 | convolution fusion | flops 1207959552 | bytes 7405568 | tf_op jit(solution)/shard_map/dot_general | solution.py:47
  35.4 0.0 reduce-scatter.3.cloned.1.call-update
  35.4 0.0 reduce-scatter.5.cloned.1.call-start
  35.4 32.2 %all-gather.2.cloned.1.call-done = bf16[1,3,256,2048]{3,2,1,0:T(8,128)(2,1)} async-done(((bf16[1,3,256,128]{3,2,1,0:T(8,128)(2,1)}), bf16[1,3,256,2048]{3,2,1,0:T(8,128)(2,1)}) %all-gather.2.cloned.1.call-update) | async-done | bytes 3145744 | tf_op jit(solution)/shard_map/all_gather | solution.py:55
  67.7 6.3 %convolution_multiply_fusion = f32[1152,2048]{1,0:T(8,128)} fusion(bf16[1,3,256,2048]{3,2,1,0:T(8,128)(2,1)} %all-gather.2.cloned.1.call-done, bf16[1,1,256,1152]{3,2,1,0:T(8,128)(2,1)S(1)} %slice_dynamic-update-slice_fusion.3), kind=kOutput, calls=%fused_computation | convolution fusion | flops 1210318848 | bytes 11075584 | tf_op jit(solution)/shard_map/dot_general | solution.py:63
  74.0 0.0 reduce-scatter.5.cloned.1.call-update
  74.0 0.0 copy-start
  74.0 6.9 %copy.6 = bf16[3,3,128,2048]{2,3,1,0:T(8,128)(2,1)} copy(bf16[3,3,128,2048]{3,2,1,0:T(8,128)(2,1)} %param.4) | data formatting | bytes 9437184 | tf_op args[1]
  80.9 5.0 %rev.3 = bf16[3,3,128,2048]{2,3,1,0:T(8,128)(2,1)} reverse(bf16[3,3,128,2048]{2,3,1,0:T(8,128)(2,1)} %copy.6), dimensions={0,1} | reverse | bytes 9437184 | tf_op jit(solution)/shard_map/rev | solution.py:54
  85.9 45.3 %reduce-scatter.3.cloned.1.call-done = f32[128,256]{0,1:T(8,128)} async-done(((f32[2048,256]{0,1:T(8,128)}), f32[128,256]{0,1:T(8,128)}) %reduce-scatter.3.cloned.1.call-update) | async-done | bytes 131088 | tf_op jit(solution)/shard_map/reduce_scatter | solution.py:46
  131.2 1.5 convert_bitcast_fusion
  132.7 0.0 copy-done
  132.7 0.3 fusion.8
  133.0 0.1 slice_dynamic-update-slice_fusion.1
  133.1 0.2 fusion.9
  133.3 0.3 fusion.10
  133.6 0.0 slice-start
  133.6 0.1 slice_dynamic-update-slice_fusion.2
  133.7 0.2 fusion.11
  133.9 0.0 slice-start.1
  134.0 0.3 fusion.12
  134.2 0.1 slice_dynamic-update-slice_fusion
  134.3 0.2 fusion.13
  134.6 1.2 slice-done
  135.8 0.2 slice-done.1
  136.0 3.2 %fusion.5 = bf16[1,1,256,128]{3,2,1,0:T(8,128)(2,1)} fusion(bf16[128,18432]{0,1:T(8,128)(2,1)S(1)} %bitcast.33, bf16[1,1,256,18432]{3,2,1,0:T(8,128)(2,1)S(1)} %fusion.13), kind=kOutput, calls=%fused_computation.11 | convolution fusion | flops 1207992320 | bytes 14221312 | tf_op jit(solution)/shard_map/dot_general | solution.py:59
  139.2 104.6 %reduce-scatter.5.cloned.1.call-done = f32[3,3,128,1024]{3,2,1,0:T(8,128)} async-done(((f32[3,3,128,2048]{3,2,1,0:T(8,128)}), f32[3,3,128,1024]{3,2,1,0:T(8,128)}) %reduce-scatter.5.cloned.1.call-update) | async-done | bytes 4718608 | tf_op jit(solution)/shard_map/reduce_scatter | solution.py:71
  (9 shorter events, 0.2 us)
Async XLA Ops:
  7.2 60.5 %all-gather.2.cloned.1.call-start = ((), (), s32[]{:S(2)}) async-start(), calls=%async_computation.3 | async-start | bytes 3342336 | tf_op jit(solution)/shard_map/all_gather | solution.py:55
  7.2 7.1 %collective-permute-start.2 = (bf16[1,1,256,128]{3,2,1,0:T(8,128)(2,1)}, bf16[1,1,256,128]{3,2,1,0:T(8,128)(2,1)S(1)}, u32[]{:S(2)}, u32[]{:S(2)}) collective-permute-start(bf16[1,1,256,128]{3,2,1,0:T(8,128)(2,1)} %param.5), channel_id=1, source_target_pairs={{0,1},{2,3},{4,5},{6,7},{8,9},{10,11},{12,13},{14,15},{16,17},{18,... | collective-permute-start | bytes 196616 | tf_op jit(solution)/shard_map/ppermute | solution.py:14
  12.1 6.4 %collective-permute-start.3 = (bf16[1,1,256,128]{3,2,1,0:T(8,128)(2,1)}, bf16[1,1,256,128]{3,2,1,0:T(8,128)(2,1)S(1)}, u32[]{:S(2)}, u32[]{:S(2)}) collective-permute-start(bf16[1,1,256,128]{3,2,1,0:T(8,128)(2,1)} %param.5), channel_id=1, source_target_pairs={{1,0},{3,2},{5,4},{7,6},{9,8},{11,10},{13,12},{15,14},{17,16},{19,... | collective-permute-start | bytes 196616 | tf_op jit(solution)/shard_map/ppermute | solution.py:15
  20.0 111.2 %reduce-scatter.3.cloned.1.call-start = ((), (), s32[]{:S(2)}) async-start(), calls=%async_computation.2 | async-start | bytes 2228224 | tf_op jit(solution)/shard_map/reduce_scatter | solution.py:46
  20.1 3.9 %collective-permute-start = (bf16[1,1,256,128]{3,2,1,0:T(8,128)(2,1)}, bf16[1,1,256,128]{3,2,1,0:T(8,128)(2,1)S(1)}, u32[]{:S(2)}, u32[]{:S(2)}) collective-permute-start(bf16[1,1,256,128]{3,2,1,0:T(8,128)(2,1)} %param.3), channel_id=1, source_target_pairs={{0,1},{2,3},{4,5},{6,7},{8,9},{10,11},{12,13},{14,15},{16,17},{18,... | collective-permute-start | bytes 196616 | tf_op jit(solution)/shard_map/ppermute | solution.py:14
  21.8 6.4 %collective-permute-start.1 = (bf16[1,1,256,128]{3,2,1,0:T(8,128)(2,1)}, bf16[1,1,256,128]{3,2,1,0:T(8,128)(2,1)S(1)}, u32[]{:S(2)}, u32[]{:S(2)}) collective-permute-start(bf16[1,1,256,128]{3,2,1,0:T(8,128)(2,1)} %param.3), channel_id=1, source_target_pairs={{1,0},{3,2},{5,4},{7,6},{9,8},{11,10},{13,12},{15,14},{17,16},{19,... | collective-permute-start | bytes 196616 | tf_op jit(solution)/shard_map/ppermute | solution.py:15
  35.4 208.4 %reduce-scatter.5.cloned.1.call-start = ((), (), s32[]{:S(2)}) async-start(), calls=%async_computation.4 | async-start | bytes 14155776 | tf_op jit(solution)/shard_map/reduce_scatter | solution.py:71
  74.0 58.7 %copy-start = (bf16[1,3,256,2048]{3,2,1,0:T(8,128)(2,1)S(1)}, bf16[1,3,256,2048]{3,2,1,0:T(8,128)(2,1)}, u32[]{:S(2)}) copy-start(bf16[1,3,256,2048]{3,2,1,0:T(8,128)(2,1)} %all-gather.2.cloned.1.call-done) | copy-start | bytes 9437188
  133.6 2.2 slice-start
  133.9 2.0 slice-start.1
Sparse Core Ops, SparseCore 0:
  20.1 47.4 all-gather.1
  71.4 59.7 reduce-scatter.2
  134.2 109.5 reduce-scatter.4
where the time goes:
time: 251 us; the launch traced here: 250 us
  waiting for transfers between devices  192 us (76%)
  local copies, waits for them, and re-layouts  16.1 us (6%)
  matrix products  14.8 us (6%)
  between operations  13.9 us (6%)
  starting transfers between devices  9.26 us (4%)
  other arithmetic  3.98 us (2%)
    reduce_scatter x1, waiting for transfers between devices, on_device(): lax.psum_scatter(scaled, 'rows', scatter_dimension=3, tiled=True)  105 us
    reduce_scatter x1, waiting for transfers between devices, on_device(): lax.psum_scatter(lax.dot_general(block, columns, contract_first, preferre...  45.3 us
    all_gather x1, waiting for transfers between devices, on_device(): piece = lax.all_gather(grad_rimmed, 'chan', axis=3, tiled=True)  32.2 us
    unnamed x23, local copies, waits for them, and re-layouts  10.8 us
    ppermute x2, waiting for transfers between devices, with_halo(): after = lax.ppermute(initial, axis, down)  8.34 us
    ppermute x2, starting transfers between devices, with_halo(): before = lax.ppermute(last, axis, up)  6.55 us
    dot_general x1, matrix products, on_device(): lax.dot_general(columns, inner, (((0,), (0,)), ((), ())), preferred_eleme...  6.29 us
    dot_general x1, matrix products, on_device(): lax.dot_general(block, columns, contract_first, preferred_element_type=jn...  5.22 us
  transfers between devices with their start and end apart: 7, of which 7 were waited for; matrix products, arithmetic and copies ran while one was open for 13% of the time, Pallas kernels for 0%

commit v1 on v0

v1 whole, which is shorter than its diff:
```python
import jax
import jax.numpy as jnp
from jax import lax
from jax.sharding import PartitionSpec as P


def taps_of(padded, height, breadth):
    return [
        padded[:, ky : ky + height, kx : kx + breadth, :].reshape(-1, padded.shape[3])
        for ky in range(3)
        for kx in range(3)
    ]


def rim(array):
    return jnp.pad(array, ((0, 0), (1, 1), (1, 1), (0, 0)))


def on_device(inputs, weights, cotangent):
    batches, height, breadth, local_ch = inputs.shape
    channels = weights.shape[3]
    groups = lax.axis_size("rows")
    row = lax.axis_index("rows")
    share = channels // groups
    total_pixels = batches * height * groups * breadth

    def around(padded):
        return lax.dynamic_slice_in_dim(padded, row * height, height + 2, axis=1)

    in_padded = rim(lax.all_gather(inputs, "rows", axis=1, tiled=True))
    cot_all = lax.all_gather(
        lax.all_gather(cotangent, "chan", axis=3, tiled=True), "rows", axis=1, tiled=True
    )
    columns = jnp.concatenate(taps_of(around(in_padded), height, breadth), axis=1)
    conv_out = lax.psum_scatter(
        lax.dot_general(
            weights.reshape(9 * local_ch, channels),
            columns,
            (((0,), (1,)), ((), ())),
            preferred_element_type=jnp.float32,
        ),
        "chan",
        scatter_dimension=0,
        tiled=True,
    )
    outputs = conv_out.T.reshape(batches, height, breadth, local_ch).astype(jnp.bfloat16)

    grad_taps = taps_of(around(rim(cot_all)), height, breadth)
    data_sum = 0.0
    for tap in range(9):
        data_sum += lax.dot_general(
            grad_taps[8 - tap],
            weights[tap // 3, tap % 3],
            (((1,), (1,)), ((), ())),
            preferred_element_type=jnp.float32,
        )
    input_grad = data_sum.reshape(batches, height, breadth, local_ch).astype(jnp.bfloat16)

    all_columns = jnp.concatenate(taps_of(in_padded, height * groups, breadth), axis=1)
    mine = lax.dynamic_slice_in_dim(cot_all, row * share, share, axis=3)
    update = lax.dot_general(
        all_columns,
        mine.reshape(total_pixels, share),
        (((0,), (0,)), ((), ())),
        preferred_element_type=jnp.float32,
    )
    weight_grad = (update / jnp.sqrt(jnp.float32(total_pixels))).reshape(3, 3, local_ch, share)
    return (outputs, input_grad, weight_grad)


def solution(mesh):
    in_specs = (
        P(None, "rows", None, "chan"),
        P(None, None, "chan", None),
        P(None, "rows", None, "chan"),
    )
    out_specs = (
        P(None, "rows", None, "chan"),
        P(None, "rows", None, "chan"),
        P(None, None, "chan", "rows"),
    )
    return jax.shard_map(
        on_device, mesh=mesh, in_specs=in_specs, out_specs=out_specs, check_vma=False
    )
```

time: 251 us -> 167 us (0.67)
  waiting for transfers between devices: 192 us -> 128 us
  local copies, waits for them, and re-layouts: 16.1 us -> 2.23 us
  starting transfers between devices: 9.26 us -> 0.12 us
  blocking collectives: 0 us -> 6.14 us
    reduce_scatter x2 -> x1, waiting for transfers between devices: 150 us -> 64.8 us  [on_device(): lax.psum_scatter(lax.dot_general(weights.reshape(9 * local_ch, channels),...]
    all_gather x1 -> x2, waiting for transfers between devices: 32.2 us -> 62.2 us  [the longest x1 32.3 us: on_device(): lax.all_gather(lax.all_gather(cotangent, 'chan', axis=3, tiled=True), 'ro...]
    unnamed x23 -> x22, local copies, waits for them, and re-layouts: 10.8 us -> 0.49 us
    ppermute x4 -> x0, waiting for transfers between devices: 10.1 us -> none  [the longest x2 8.34 us: with_halo(): after = lax.ppermute(initial, axis, down)]
    ppermute x4 -> x0, starting transfers between devices: 9.14 us -> none  [the longest x2 6.55 us: with_halo(): before = lax.ppermute(last, axis, up)]
    all_gather x0 -> x1, blocking collectives: none -> 6.14 us  [on_device(): in_padded = rim(lax.all_gather(inputs, 'rows', axis=1, tiled=True))]
    rev x1 -> x0, local copies, waits for them, and re-layouts: 4.99 us -> none  [on_device(): flipped = jnp.transpose(weights[::-1, ::-1], (2, 0, 1, 3))]
    dot_general x3 -> x11, matrix products: 14.8 us -> 14.9 us  [the longest x9 6.04 us: on_device(): lax.dot_general(grad_taps[8 - tap], weights[tap // 3, tap % 3], (((1,), (...]
  transfers between devices with their start and end apart: 7 -> 3, of which waited for: 7 -> 3; matrix products, arithmetic and copies ran while one was open for 13% -> 5% of each run, Pallas kernels for 0% -> 0%
where the time goes in v1:
time: 167 us
  waiting for transfers between devices  128 us (77%)
  matrix products  14.9 us (9%)
  between operations  14 us (8%)
  blocking collectives  6.14 us (4%)
  local copies, waits for them, and re-layouts  2.23 us (1%)
    reduce_scatter x1, waiting for transfers between devices, on_device(): lax.psum_scatter(lax.dot_general(weights.reshape(9 * local_ch, channels),...  64.8 us
    all_gather x1, waiting for transfers between devices, on_device(): lax.all_gather(lax.all_gather(cotangent, 'chan', axis=3, tiled=True), 'ro...  32.3 us
    all_gather x1, waiting for transfers between devices, on_device(): lax.all_gather(cotangent, 'chan', axis=3, tiled=True)  29.9 us
    all_gather x1, blocking collectives, on_device(): in_padded = rim(lax.all_gather(inputs, 'rows', axis=1, tiled=True))  6.14 us
    dot_general x9, matrix products, on_device(): lax.dot_general(grad_taps[8 - tap], weights[tap // 3, tap % 3], (((1,), (...  6.04 us
    dot_general x1, matrix products, on_device(): lax.dot_general(weights.reshape(9 * local_ch, channels), columns, (((0,),...  5.23 us
    dot_general x1, matrix products, on_device(): lax.dot_general(all_columns, mine.reshape(total_pixels, share), (((0,), (...  3.62 us
  transfers between devices with their start and end apart: 3, of which 3 were waited for; matrix products, arithmetic and copies ran while one was open for 5% of the time, Pallas kernels for 0%

profile of v1, /device:TPU:0, one launch (start us, length us, event | category | flops | bytes accessed | tf_op | source)
XLA Modules:
  0.0 166.6 jit_solution(7292825136925069916)
XLA Ops:
  7.2 0.0 all-gather.3.cloned.1.call-start
  7.2 0.7 all-gather.3.cloned.1.call-update
  7.9 0.0 reduce-scatter.2.cloned.1.call-start
  7.9 6.1 %all_gather.9 = bf16[1,2,256,128]{3,2,0,1:T(8,128)(2,1)S(1)} all-gather(bf16[1,1,256,128]{3,2,0,1:T(8,128)(2,1)} %bitcast.139), channel_id=1, replica_groups=mesh['chan'=16,'rows'=2] {'rows'}, dimensions={1}, use_global_device_ids=true | all-gather | bytes 196608 | tf_op jit(solution)/shard_map/all_gather | solution.py:30
  14.1 0.1 fusion.39
  14.4 0.1 fusion.41
  14.5 5.2 %convolution_bitcast_fusion = f32[2048,256]{0,1:T(8,128)} fusion(bf16[256,1152]{1,0:T(8,128)(2,1)S(1)} %fusion.41, bf16[1152,2048]{1,0:T(8,128)(2,1)} %bitcast.126), kind=kOutput, calls=%fused_computation.10 | convolution fusion | flops 1207959552 | bytes 7405568 | tf_op jit(solution)/shard_map/dot_general | solution.py:36
  19.7 0.0 reduce-scatter.2.cloned.1.call-update
  19.7 0.0 all-gather.5.cloned.1.call-start
  19.8 29.9 %all-gather.3.cloned.1.call-done = bf16[1,1,256,2048]{3,2,0,1:T(8,128)(2,1)} async-done(((bf16[1,1,256,128]{3,2,0,1:T(8,128)(2,1)}), bf16[1,1,256,2048]{3,2,0,1:T(8,128)(2,1)}) %all-gather.3.cloned.1.call-update) | async-done | bytes 1048592 | tf_op jit(solution)/shard_map/all_gather | solution.py:32
  49.7 0.0 all-gather.5.cloned.1.call-update
  49.7 0.1 pad_slice_fusion
  50.2 64.8 %reduce-scatter.2.cloned.1.call-done = f32[128,256]{0,1:T(8,128)} async-done(((f32[2048,256]{0,1:T(8,128)}), f32[128,256]{0,1:T(8,128)}) %reduce-scatter.2.cloned.1.call-update) | async-done | bytes 131088 | tf_op jit(solution)/shard_map/reduce_scatter | solution.py:35
  115.0 1.5 convert_bitcast_fusion
  116.6 32.3 %all-gather.5.cloned.1.call-done = bf16[1,2,256,2048]{3,2,0,1:T(8,128)(2,1)} async-done(((bf16[1,1,256,2048]{3,2,0,1:T(8,128)(2,1)}), bf16[1,2,256,2048]{3,2,0,1:T(8,128)(2,1)}) %all-gather.5.cloned.1.call-update) | async-done | bytes 2097168 | tf_op jit(solution)/shard_map/all_gather | solution.py:31
  148.9 0.0 slice-start
  148.9 1.4 constant_dynamic-slice_fusion
  150.3 0.0 copy-start
  150.3 0.0 slice-start.1
  150.3 3.6 %convolution_multiply_fusion = f32[1152,1024]{1,0:T(8,128)} fusion(bf16[512,1152]{1,0:T(8,128)(2,1)S(1)} %constant_dynamic-update-slice_fusion, bf16[512,1024]{1,0:T(8,128)(2,1)S(1)} %bitcast.129), kind=kOutput, calls=%fused_computation.9 | convolution fusion | flops 1209139200 | bytes 6946816 | tf_op jit(solution)/shard_map/dot_general | solution.py:61
  154.0 0.0 copy-done
  154.0 1.5 fusion.19
  155.5 0.0 slice-done
  155.5 0.0 slice-done.1
  155.5 0.5 convolution_add_fusion.7
  156.0 0.5 convolution_add_fusion.6
  156.5 0.5 convolution_add_fusion.5
  157.0 0.4 convolution_add_fusion.4
  157.5 0.5 convolution_add_fusion.3
  158.0 0.5 convolution_add_fusion.2
  158.5 0.4 convolution_add_fusion.1
  158.9 1.1 fusion.1
  (18 shorter events, 0.5 us)
Async XLA Ops:
  7.2 42.5 %all-gather.3.cloned.1.call-start = ((), (), s32[]{:S(2)}) async-start(), calls=%async_computation.2 | async-start | bytes 1114112 | tf_op jit(solution)/shard_map/all_gather | solution.py:32
  7.9 107.1 %reduce-scatter.2.cloned.1.call-start = ((), (), s32[]{:S(2)}) async-start(), calls=%async_computation.1 | async-start | bytes 2228224 | tf_op jit(solution)/shard_map/reduce_scatter | solution.py:35
  19.7 129.1 %all-gather.5.cloned.1.call-start = ((), (), s32[]{:S(2)}) async-start(), calls=%async_computation.3 | async-start | bytes 3145728 | tf_op jit(solution)/shard_map/all_gather | solution.py:31
  148.9 6.6 %slice-start = ((s8[4718592]{0:T(1024)(128)(4,1)}), s8[4194304]{0:T(1024)(128)(4,1)S(1)}, s32[]{:S(2)}) async-start(s8[4718592]{0:T(1024)(128)(4,1)} %bitcast.127), calls=%async_computation.4 | async-start | bytes 8388608
  150.3 3.7 %copy-start = (bf16[1,2,256,2048]{3,2,0,1:T(8,128)(2,1)S(1)}, bf16[1,2,256,2048]{3,2,0,1:T(8,128)(2,1)}, u32[]{:S(2)}) copy-start(bf16[1,2,256,2048]{3,2,0,1:T(8,128)(2,1)} %all-gather.5.cloned.1.call-done) | copy-start | bytes 6291460
  150.3 5.2 %slice-start.1 = ((s8[4718592]{0:T(1024)(128)(4,1)}), s8[524288]{0:T(1024)(128)(4,1)S(1)}, s32[]{:S(2)}) async-start(s8[4718592]{0:T(1024)(128)(4,1)} %bitcast.127), calls=%async_computation.5 | async-start | bytes 1048576
Sparse Core Ops, SparseCore 0:
  10.2 39.4 all-gather.2
  54.0 60.9 reduce-scatter.1
  116.7 32.1 all-gather.4

commit v2 on v1

--- a/solution.py
+++ b/solution.py
@@ -1,7 +1,256 @@
+import functools
+
 import jax
 import jax.numpy as jnp
 from jax import lax
+from jax.experimental import pallas as pl
+from jax.experimental.pallas import tpu as pltpu
 from jax.sharding import PartitionSpec as P
+
+F32 = jnp.float32
+BF16 = jnp.bfloat16
+ZS = 4
+
+
+def moved(value, step):
+    rows = value.shape[0]
+    rolled = pltpu.roll(value, step % rows, 0)
+    at = lax.broadcasted_iota(jnp.int32, value.shape, 0)
+    edge = 0 if step == 1 else rows - 1
+    return jnp.where(at == edge, 0.0, rolled)
+
+
+def fused_kernel(
+    scale, x_ref, cot_ref, w_hbm, out_ref, igrad_ref, wgrad_hbm,
+    w_ref, x_all, cols, cot_all, keep, sib_out, sib_in, x_out, x_in, z_out, z_in, wg,
+    in_send, in_recv, cot_send, cot_recv, sib_send, sib_recv, x_send, x_recv,
+    z_send, z_recv, w_sem, wg_sem,
+):
+    chan = lax.axis_index("chan")
+    y = lax.axis_index("rows")
+    core = chan % 2
+    x = (chan // 2) % 2
+    z = chan // 4
+    deep = x_ref.shape[1]
+    channels = w_ref.shape[1]
+
+    def chan_of(zz, xx, cc):
+        return zz * 4 + xx * 2 + cc
+
+    def device(ch, row):
+        return {"chan": ch, "rows": row}
+
+    sibling = device(chan_of(z, x, 1 - core), y)
+    x_peer = device(chan_of(z, 1 - x, core), y)
+    y_peer = device(chan, 1 - y)
+    z_at = [(z + k) % ZS for k in range(ZS)]
+    z_peers = [device(chan_of(z_at[k], x, core), y) for k in range(1, ZS)]
+
+    loads = []
+    for part in range(3):
+        rows = pl.ds(part * 3 * deep, 3 * deep)
+        load = pltpu.make_async_copy(w_hbm.at[rows], w_ref.at[rows], w_sem.at[part])
+        load.start()
+        loads.append(load)
+
+    barrier = pltpu.get_barrier_semaphore()
+    peers = [sibling, x_peer, y_peer] + z_peers
+    for peer in peers:
+        pl.semaphore_signal(barrier, 1, device_id=peer, device_id_type=pl.DeviceIdType.MESH)
+    pl.semaphore_wait(barrier, len(peers))
+
+    pending = []
+
+    def send(src, dst, send_sem, recv_sem, to):
+        copy = pltpu.make_async_remote_copy(
+            src_ref=src, dst_ref=dst, send_sem=send_sem, recv_sem=recv_sem,
+            device_id=to, device_id_type=pl.DeviceIdType.MESH,
+        )
+        copy.start()
+        pending.append(copy)
+        return copy
+
+    in_copy = send(x_ref, x_all.at[y], in_send, in_recv.at[y], y_peer)
+    x_all[y] = x_ref[...]
+
+    def block(row, ch):
+        return cot_all.at[row, :, pl.ds(pl.multiple_of(ch * deep, deep), deep)]
+
+    count = [0]
+
+    def pass_on(src, row, ch, to):
+        send(src, block(row, ch), cot_send.at[count[0]], cot_recv.at[row, ch], to)
+        count[0] += 1
+
+    def arrived(row, ch):
+        pltpu.make_async_remote_copy(
+            src_ref=block(row, ch), dst_ref=block(row, ch), send_sem=cot_send.at[0],
+            recv_sem=cot_recv.at[row, ch], device_id=sibling,
+            device_id_type=pl.DeviceIdType.MESH,
+        ).wait_recv()
+
+    for k in (2, 1, 3):
+        pass_on(cot_ref, y, chan, z_peers[k - 1])
+    pass_on(cot_ref, y, chan, x_peer)
+    pass_on(cot_ref, y, chan, y_peer)
+    pass_on(cot_ref, y, chan, sibling)
+    block(y, chan)[...] = cot_ref[...]
+
+    pltpu.make_async_remote_copy(
+        src_ref=x_all.at[1 - y], dst_ref=x_all.at[1 - y], send_sem=in_send,
+        recv_sem=in_recv.at[1 - y], device_id=y_peer, device_id_type=pl.DeviceIdType.MESH,
+    ).wait_recv()
+    for row in range(2):
+        line = x_all[row].astype(F32)
+        base = row * 3 * deep
+        cols[:, base : base + deep] = moved(line, 1).astype(BF16)
+        cols[:, base + deep : base + 2 * deep] = x_all[row]
+        cols[:, base + 2 * deep : base + 3 * deep] = moved(line, -1).astype(BF16)
+    for load in loads:
+        load.wait()
+
+    slab = pl.ds(pl.multiple_of((1 - y) * (3 * deep), deep), 6 * deep)
+
+    def conv_chunk(index):
+        zz = z_at[(index + 1) % ZS]
+        xx = 1 - x if index < ZS else x
+        start = pl.multiple_of((zz * 2 + xx) * (2 * deep), 2 * deep)
+        part = jnp.dot(cols[...], w_ref[slab, pl.ds(start, 2 * deep)], preferred_element_type=F32)
+        low, high = part[:, :deep], part[:, deep:]
+        mine = core == 0
+        keep[index] = jnp.where(mine, low, high)
+        sib_out[index] = jnp.where(mine, high, low)
+        return send(sib_out.at[index], sib_in.at[index], sib_send.at[index], sib_recv.at[index], sibling)
+
+    sib_copies = [conv_chunk(i) for i in range(ZS)]
+
+    for k in (1, 3, 2):
+        ch = chan_of(z_at[k], x, core)
+        arrived(y, ch)
+        for to in (x_peer, y_peer, sibling):
+            pass_on(block(y, ch), y, ch, to)
+
+    x_copies = []
+    for i in range(ZS):
+        sib_copies[i].wait_recv()
+        x_out[i] = keep[i] + sib_in[i]
+        x_copies.append(send(x_out.at[i], x_in.at[i], x_send.at[i], x_recv.at[i], x_peer))
+
+    sib_copies += [conv_chunk(i) for i in range(ZS, 2 * ZS)]
+
+    for k in (0, 1, 3, 2):
+        ch = chan_of(z_at[k], 1 - x, core)
+        arrived(y, ch)
+        for to in (y_peer, sibling):
+            pass_on(block(y, ch), y, ch, to)
+
+    z_copies = []
+    for i in range(ZS):
+        sib_copies[ZS + i].wait_recv()
+        x_copies[i].wait_recv()
+        z_out[i] = keep[ZS + i] + sib_in[ZS + i] + x_in[i]
+        if i < ZS - 1:
+            z_copies.append(send(z_out.at[i], z_in.at[i], z_send.at[i], z_recv.at[i], z_peers[i]))
+
+    for xx in (x, 1 - x):
+        for k in (0, 1, 3, 2):
+            ch = chan_of(z_at[k], xx, core)
+            arrived(1 - y, ch)
+            pass_on(block(1 - y, ch), 1 - y, ch, sibling)
+    for row in (y, 1 - y):
+        for xx in (x, 1 - x):
+            for k in range(ZS):
+                arrived(row, chan_of(z_at[k], xx, 1 - core))
+
+    share = channels // 2
+    half = pl.ds(pl.multiple_of(y * share, share), share)
+    first = (((0,), (0,)), ((), ()))
+    stores = []
+    for ky in range(3):
+        total = None
+        for row in range(2):
+            other = row - ky + 1
+            if 0 <= other < 2:
+                term = lax.dot_general(
+                    cols[:, row * 3 * deep : (row + 1) * 3 * deep], cot_all[other, :, half],
+                    first, preferred_element_type=F32,
+                )
+                total = term if total is None else total + term
+        rows = pl.ds(ky * 3 * deep, 3 * deep)
+        wg[rows] = total * scale
+        store = pltpu.make_async_copy(wg.at[rows], wgrad_hbm.at[rows], wg_sem.at[ky])
+        store.start()
+        stores.append(store)
+
+    second = (((1,), (1,)), ((), ()))
+    spread = None
+    for row in range(2):
+        rows = pl.ds(pl.multiple_of((y - row + 1) * (3 * deep), deep), 3 * deep)
+        term = lax.dot_general(cot_all[row], w_ref[rows], second, preferred_element_type=F32)
+        spread = term if spread is None else spread + term
+    igrad_ref[...] = (
+        moved(spread[:, :deep], -1) + spread[:, deep : 2 * deep] + moved(spread[:, 2 * deep :], 1)
+    ).astype(BF16)
+
+    total = z_out[ZS - 1]
+    for i in range(ZS - 1):
+        z_copies[i].wait_recv()
+        total = total + z_in[i]
+    out_ref[...] = total.astype(BF16)
+    for copy in pending:
+        copy.wait_send()
+    for store in stores:
+        store.wait()
+
+
+def fused(inputs, weights, cotangent):
+    breadth, deep = inputs.shape[2:]
+    channels = weights.shape[3]
+    share = channels // 2
+    total_pixels = 2 * breadth
+    vmem = pl.BlockSpec(memory_space=pltpu.VMEM)
+    hbm = pl.BlockSpec(memory_space=pl.ANY)
+    dma = pltpu.SemaphoreType.DMA
+    tile = (breadth, deep)
+    outs = pl.pallas_call(
+        functools.partial(fused_kernel, float(total_pixels) ** -0.5),
+        out_shape=[
+            jax.ShapeDtypeStruct(tile, BF16),
+            jax.ShapeDtypeStruct(tile, BF16),
+            jax.ShapeDtypeStruct((9 * deep, share), F32),
+        ],
+        in_specs=[vmem, vmem, hbm],
+        out_specs=[vmem, vmem, hbm],
+        scratch_shapes=[
+            pltpu.VMEM((9 * deep, channels), BF16),
+            pltpu.VMEM((2,) + tile, BF16),
+            pltpu.VMEM((breadth, 6 * deep), BF16),
+            pltpu.VMEM((2, breadth, channels), BF16),
+            pltpu.VMEM((2 * ZS,) + tile, F32),
+            pltpu.VMEM((2 * ZS,) + tile, F32),
+            pltpu.VMEM((2 * ZS,) + tile, F32),
+            pltpu.VMEM((ZS,) + tile, F32),
+            pltpu.VMEM((ZS,) + tile, F32),
+            pltpu.VMEM((ZS,) + tile, F32),
+            pltpu.VMEM((ZS - 1,) + tile, F32),
+            pltpu.VMEM((9 * deep, share), F32),
+            dma, dma((2,)), dma((31,)), dma((2, 16)), dma((2 * ZS,)), dma((2 * ZS,)),
+            dma((ZS,)), dma((ZS,)), dma((ZS - 1,)), dma((ZS - 1,)), dma((3,)), dma((3,)),
+        ],
+        compiler_params=pltpu.CompilerParams(
+            collective_id=0, has_side_effects=True, vmem_limit_bytes=44 * 1024 * 1024
+        ),
+        cost_estimate=pl.CostEstimate(
+            flops=2 * 3 * 9 * deep * channels * breadth,
+            bytes_accessed=2 * 9 * deep * channels + 4 * 9 * deep * share,
+            transcendentals=0,
+        ),
+    )(inputs.reshape(tile), cotangent.reshape(tile), weights.reshape(9 * deep, channels))
+    return (
+        outs[0].reshape(inputs.shape),
+        outs[1].reshape(inputs.shape),
+        outs[2].reshape(3, 3, deep, share),
+    )
 
 
 def taps_of(padded, height, breadth):
@@ -20,6 +269,8 @@
     batches, height, breadth, local_ch = inputs.shape
     channels = weights.shape[3]
     groups = lax.axis_size("rows")
+    if (groups, lax.axis_size("chan"), height, batches) == (2, 16, 1, 1):
+        return fused(inputs, weights, cotangent)
     row = lax.axis_index("rows")
     share = channels // groups
     total_pixels = batches * height * groups * breadth

time: 167 us -> 41.4 us (0.25)
  waiting for transfers between devices: 128 us -> 0 us
  Pallas kernels: 0 us -> 32.6 us
  matrix products: 14.9 us -> 0 us
  between operations: 14 us -> 0.65 us
  blocking collectives: 6.14 us -> 0 us
  local copies, waits for them, and re-layouts: 2.23 us -> 7.45 us
    reduce_scatter x1 -> x0, waiting for transfers between devices: 64.8 us -> none  [on_device(): lax.psum_scatter(lax.dot_general(weights.reshape(9 * local_ch, channels),...]
    all_gather x2 -> x0, waiting for transfers between devices: 62.2 us -> none  [the longest x1 32.3 us: on_device(): lax.all_gather(lax.all_gather(cotangent, 'chan', axis=3, tiled=True), 'ro...]
    pallas_call x0 -> x1, Pallas kernels: none -> 32.6 us  [fused(): pl.pallas_call(functools.partial(fused_kernel, float(total_pixels) ** (-0...]
    dot_general x11 -> x0, matrix products: 14.9 us -> none  [the longest x9 6.04 us: on_device(): lax.dot_general(grad_taps[8 - tap], weights[tap // 3, tap % 3], (((1,), (...]
    unnamed x22 -> x9, local copies, waits for them, and re-layouts: 0.49 us -> 7.45 us
    all_gather x1 -> x0, blocking collectives: 6.14 us -> none  [on_device(): in_padded = rim(lax.all_gather(inputs, 'rows', axis=1, tiled=True))]
  transfers between devices with their start and end apart: 3 -> 0, of which waited for: 3 -> 0; matrix products, arithmetic and copies ran while one was open for 5% -> 0% of each run, Pallas kernels for 0% -> 0%
where the time goes in v2:
time: 41.4 us; the launch traced here: 40.7 us
  Pallas kernels  32.6 us (79%)
  local copies, waits for them, and re-layouts  7.45 us (18%)
  between operations  0.65 us (2%)
    pallas_call x1, Pallas kernels, fused(): pl.pallas_call(functools.partial(fused_kernel, float(total_pixels) ** (-0...  32.6 us
    unnamed x9, local copies, waits for them, and re-layouts  7.45 us

profile of v2, /device:TPU:0, one launch (start us, length us, event | category | flops | bytes accessed | tf_op | source)
XLA Modules:
  0.0 40.7 jit_solution(5600813431458278906)
XLA Ops:
  0.6 0.0 copy-start
  0.6 2.3 %copy-done = bf16[3,3,128,2048]{3,2,1,0:T(8,128)(2,1)S(1)} copy-done((bf16[3,3,128,2048]{3,2,1,0:T(8,128)(2,1)S(1)}, bf16[3,3,128,2048]{3,2,1,0:T(8,128)(2,1)}, u32[]{:S(2)}) %copy-start) | copy-done | bytes 4718616
  3.0 0.0 copy-start.1
  3.0 0.8 %copy-done.1 = bf16[1,1,256,128]{3,2,1,0:T(8,128)(2,1)S(1)} copy-done((bf16[1,1,256,128]{3,2,1,0:T(8,128)(2,1)S(1)}, bf16[1,1,256,128]{3,2,1,0:T(8,128)(2,1)}, u32[]{:S(2)}) %copy-start.1) | copy-done | bytes 65560
  3.8 0.0 copy-start.2
  3.8 0.8 %copy-done.2 = bf16[1,1,256,128]{3,2,1,0:T(8,128)(2,1)S(1)} copy-done((bf16[1,1,256,128]{3,2,1,0:T(8,128)(2,1)S(1)}, bf16[1,1,256,128]{3,2,1,0:T(8,128)(2,1)}, u32[]{:S(2)}) %copy-start.2) | copy-done | bytes 65560
  4.6 32.6 %shard_map.58 = (bf16[256,128]{1,0:T(8,128)(2,1)S(1)}, bf16[256,128]{1,0:T(8,128)(2,1)S(1)}, f32[1152,1024]{1,0:T(8,128)S(1)}) custom-call(bf16[256,128]{1,0:T(8,128)(2,1)S(1)} %bitcast.10, bf16[256,128]{1,0:T(8,128)(2,1)S(1)} %bitcast.11, bf16[1152,2048]{1,0:T(8,128)(2,1)S(1)} %bitcast.9), custom_call_target="tpu_custom_call" | custom-call | flops 3623878656 | bytes 9437184 | tf_op jit(solution)/shard_map/pallas_call | solution.py:215
  37.2 0.6 %copy.9 = bf16[1,1,256,128]{3,2,1,0:T(8,128)(2,1)} copy(bf16[1,1,256,128]{3,2,1,0:T(8,128)(2,1)S(1)} %bitcast.8) | data formatting | bytes 131072
  37.9 0.6 %copy.10 = bf16[1,1,256,128]{3,2,1,0:T(8,128)(2,1)} copy(bf16[1,1,256,128]{3,2,1,0:T(8,128)(2,1)S(1)} %bitcast.7) | data formatting | bytes 131072
  38.5 2.2 %copy.11 = f32[3,3,128,1024]{3,2,1,0:T(8,128)} copy(f32[3,3,128,1024]{3,2,1,0:T(8,128)S(1)} %bitcast.6) | data formatting | bytes 9437184
Async XLA Ops:
  0.6 2.3 %copy-start = (bf16[3,3,128,2048]{3,2,1,0:T(8,128)(2,1)S(1)}, bf16[3,3,128,2048]{3,2,1,0:T(8,128)(2,1)}, u32[]{:S(2)}) copy-start(bf16[3,3,128,2048]{3,2,1,0:T(8,128)(2,1)} %param.4) | copy-start | bytes 14155780
  3.0 0.8 %copy-start.1 = (bf16[1,1,256,128]{3,2,1,0:T(8,128)(2,1)S(1)}, bf16[1,1,256,128]{3,2,1,0:T(8,128)(2,1)}, u32[]{:S(2)}) copy-start(bf16[1,1,256,128]{3,2,1,0:T(8,128)(2,1)} %param.3) | copy-start | bytes 196612
  3.8 0.8 %copy-start.2 = (bf16[1,1,256,128]{3,2,1,0:T(8,128)(2,1)S(1)}, bf16[1,1,256,128]{3,2,1,0:T(8,128)(2,1)}, u32[]{:S(2)}) copy-start(bf16[1,1,256,128]{3,2,1,0:T(8,128)(2,1)} %param.5) | copy-start | bytes 196612

commit v3 on v2

--- a/solution.py
+++ b/solution.py
@@ -24,7 +24,7 @@
     scale, x_ref, cot_ref, w_hbm, out_ref, igrad_ref, wgrad_hbm,
     w_ref, x_all, cols, cot_all, keep, sib_out, sib_in, x_out, x_in, z_out, z_in, wg,
     in_send, in_recv, cot_send, cot_recv, sib_send, sib_recv, x_send, x_recv,
-    z_send, z_recv, w_sem, wg_sem,
+    z_send, z_recv, w_sem, wg_sem, own_sem,
 ):
     chan = lax.axis_index("chan")
     y = lax.axis_index("rows")
@@ -34,6 +34,14 @@
     deep = x_ref.shape[1]
     channels = w_ref.shape[1]
 
+    def block(row, ch):
+        return cot_all.at[row, :, pl.ds(pl.multiple_of(ch * deep, deep), deep)]
+
+    own_x = pltpu.make_async_copy(x_ref, x_all.at[y], own_sem.at[0])
+    own_x.start()
+    own_cot = pltpu.make_async_copy(cot_ref, block(y, chan), own_sem.at[1])
+    own_cot.start()
+
     def chan_of(zz, xx, cc):
         return zz * 4 + xx * 2 + cc
 
@@ -71,10 +79,6 @@
         return copy
 
     in_copy = send(x_ref, x_all.at[y], in_send, in_recv.at[y], y_peer)
-    x_all[y] = x_ref[...]
-
-    def block(row, ch):
-        return cot_all.at[row, :, pl.ds(pl.multiple_of(ch * deep, deep), deep)]
 
     count = [0]
 
@@ -94,7 +98,8 @@
     pass_on(cot_ref, y, chan, x_peer)
     pass_on(cot_ref, y, chan, y_peer)
     pass_on(cot_ref, y, chan, sibling)
-    block(y, chan)[...] = cot_ref[...]
+    own_x.wait()
+    own_cot.wait()
 
     pltpu.make_async_remote_copy(
         src_ref=x_all.at[1 - y], dst_ref=x_all.at[1 - y], send_sem=in_send,
@@ -130,33 +135,33 @@
         for to in (x_peer, y_peer, sibling):
             pass_on(block(y, ch), y, ch, to)
 
+    sib_copies += [conv_chunk(i) for i in range(ZS, 2 * ZS)]
+
     x_copies = []
     for i in range(ZS):
         sib_copies[i].wait_recv()
         x_out[i] = keep[i] + sib_in[i]
         x_copies.append(send(x_out.at[i], x_in.at[i], x_send.at[i], x_recv.at[i], x_peer))
 
-    sib_copies += [conv_chunk(i) for i in range(ZS, 2 * ZS)]
-
     for k in (0, 1, 3, 2):
         ch = chan_of(z_at[k], 1 - x, core)
         arrived(y, ch)
         for to in (y_peer, sibling):
             pass_on(block(y, ch), y, ch, to)
 
+    order = [(k, xx) for xx in (x, 1 - x) for k in (0, 1, 3, 2)]
     z_copies = []
     for i in range(ZS):
+        for k, xx in order[2 * i : 2 * i + 2]:
+            ch = chan_of(z_at[k], xx, core)
+            arrived(1 - y, ch)
+            pass_on(block(1 - y, ch), 1 - y, ch, sibling)
         sib_copies[ZS + i].wait_recv()
         x_copies[i].wait_recv()
         z_out[i] = keep[ZS + i] + sib_in[ZS + i] + x_in[i]
         if i < ZS - 1:
             z_copies.append(send(z_out.at[i], z_in.at[i], z_send.at[i], z_recv.at[i], z_peers[i]))
 
-    for xx in (x, 1 - x):
-        for k in (0, 1, 3, 2):
-            ch = chan_of(z_at[k], xx, core)
-            arrived(1 - y, ch)
-            pass_on(block(1 - y, ch), 1 - y, ch, sibling)
     for row in (y, 1 - y):
         for xx in (x, 1 - x):
             for k in range(ZS):
@@ -209,7 +214,7 @@
     share = channels // 2
     total_pixels = 2 * breadth
     vmem = pl.BlockSpec(memory_space=pltpu.VMEM)
-    hbm = pl.BlockSpec(memory_space=pl.ANY)
+    hbm = pl.BlockSpec(memory_space=pltpu.HBM)
     dma = pltpu.SemaphoreType.DMA
     tile = (breadth, deep)
     outs = pl.pallas_call(
@@ -219,7 +224,7 @@
             jax.ShapeDtypeStruct(tile, BF16),
             jax.ShapeDtypeStruct((9 * deep, share), F32),
         ],
-        in_specs=[vmem, vmem, hbm],
+        in_specs=[hbm, hbm, hbm],
         out_specs=[vmem, vmem, hbm],
         scratch_shapes=[
             pltpu.VMEM((9 * deep, channels), BF16),
@@ -235,10 +240,10 @@
             pltpu.VMEM((ZS - 1,) + tile, F32),
             pltpu.VMEM((9 * deep, share), F32),
             dma, dma((2,)), dma((31,)), dma((2, 16)), dma((2 * ZS,)), dma((2 * ZS,)),
-            dma((ZS,)), dma((ZS,)), dma((ZS - 1,)), dma((ZS - 1,)), dma((3,)), dma((3,)),
+            dma((ZS,)), dma((ZS,)), dma((ZS - 1,)), dma((ZS - 1,)), dma((3,)), dma((3,)), dma((2,)),
         ],
         compiler_params=pltpu.CompilerParams(
-            collective_id=0, has_side_effects=True, vmem_limit_bytes=44 * 1024 * 1024
+            collective_id=0, has_side_effects=True, vmem_limit_bytes=60 * 1024 * 1024
         ),
         cost_estimate=pl.CostEstimate(
             flops=2 * 3 * 9 * deep * channels * breadth,

time: 41.4 us -> 42.3 us (1.022); the launches traced: 40.7 us -> 42 us
  local copies, waits for them, and re-layouts: 7.45 us -> 8.19 us
  Pallas kernels: 32.6 us -> 33.2 us
    unnamed x9 -> x3, local copies, waits for them, and re-layouts: 7.45 us -> 8.19 us
    pallas_call x1, Pallas kernels: 32.6 us -> 33.2 us  [fused(): pl.pallas_call(functools.partial(fused_kernel, float(total_pixels) ** (-0...]
where the time goes in v3:
time: 42.3 us; the launch traced here: 42 us
  Pallas kernels  33.2 us (78%)
  local copies, waits for them, and re-layouts  8.19 us (19%)
  between operations  0.64 us (2%)
    pallas_call x1, Pallas kernels, fused(): pl.pallas_call(functools.partial(fused_kernel, float(total_pixels) ** (-0...  33.2 us
    unnamed x3, local copies, waits for them, and re-layouts  8.19 us

profile of v3, /device:TPU:0, one launch (start us, length us, event | category | flops | bytes accessed | tf_op | source)
XLA Modules:
  0.0 42.0 jit_solution(11508529203697392794)
XLA Ops:
  0.6 33.2 %shard_map.58 = (bf16[256,128]{1,0:T(8,128)(2,1)}, bf16[256,128]{1,0:T(8,128)(2,1)}, f32[1152,1024]{1,0:T(8,128)}) custom-call(bf16[256,128]{1,0:T(8,128)(2,1)} %bitcast.10, bf16[256,128]{1,0:T(8,128)(2,1)} %bitcast.11, bf16[1152,2048]{1,0:T(8,128)(2,1)} %bitcast.9), custom_call_target="tpu_custom_call" | custom-call | flops 3623878656 | bytes 9437184 | tf_op jit(solution)/shard_map/pallas_call | solution.py:220
  33.8 1.5 %copy.9 = bf16[1,1,256,128]{3,2,1,0:T(8,128)(2,1)} copy(bf16[1,1,256,128]{3,2,1,0:T(8,128)(2,1)} %bitcast.8) | data formatting | bytes 131072
  35.3 1.5 %copy.10 = bf16[1,1,256,128]{3,2,1,0:T(8,128)(2,1)} copy(bf16[1,1,256,128]{3,2,1,0:T(8,128)(2,1)} %bitcast.7) | data formatting | bytes 131072
  36.8 5.2 %copy.11 = f32[3,3,128,1024]{3,2,1,0:T(8,128)} copy(f32[3,3,128,1024]{3,2,1,0:T(8,128)} %bitcast.6) | data formatting | bytes 9437184

commit v4 on v3

--- a/solution.py
+++ b/solution.py
@@ -21,10 +21,10 @@
 
 
 def fused_kernel(
-    scale, x_ref, cot_ref, w_hbm, out_ref, igrad_ref, wgrad_hbm,
-    w_ref, x_all, cols, cot_all, keep, sib_out, sib_in, x_out, x_in, z_out, z_in, wg,
+    x_ref, cot_ref, w_hbm, out_ref, igrad_ref, cols_hbm, half_hbm,
+    w_ref, x_all, cols, cot_all, keep, sib_out, sib_in, x_out, x_in, z_out, z_in,
     in_send, in_recv, cot_send, cot_recv, sib_send, sib_recv, x_send, x_recv,
-    z_send, z_recv, w_sem, wg_sem, own_sem,
+    z_send, z_recv, w_sem, out_sem, own_sem,
 ):
     chan = lax.axis_index("chan")
     y = lax.axis_index("rows")
@@ -111,6 +111,15 @@
         cols[:, base : base + deep] = moved(line, 1).astype(BF16)
         cols[:, base + deep : base + 2 * deep] = x_all[row]
         cols[:, base + 2 * deep : base + 3 * deep] = moved(line, -1).astype(BF16)
+    kept_cols = pltpu.make_async_copy(cols, cols_hbm, out_sem.at[0])
+    kept_cols.start()
+
+    for k in (1, 3, 2):
+        ch = chan_of(z_at[k], x, core)
+        arrived(y, ch)
+        for to in (x_peer, y_peer, sibling):
+            pass_on(block(y, ch), y, ch, to)
+
     for load in loads:
         load.wait()
 
@@ -128,12 +137,6 @@
         return send(sib_out.at[index], sib_in.at[index], sib_send.at[index], sib_recv.at[index], sibling)
 
     sib_copies = [conv_chunk(i) for i in range(ZS)]
-
-    for k in (1, 3, 2):
-        ch = chan_of(z_at[k], x, core)
-        arrived(y, ch)
-        for to in (x_peer, y_peer, sibling):
-            pass_on(block(y, ch), y, ch, to)
 
     sib_copies += [conv_chunk(i) for i in range(ZS, 2 * ZS)]
 
@@ -169,23 +172,8 @@
 
     share = channels // 2
     half = pl.ds(pl.multiple_of(y * share, share), share)
-    first = (((0,), (0,)), ((), ()))
-    stores = []
-    for ky in range(3):
-        total = None
-        for row in range(2):
-            other = row - ky + 1
-            if 0 <= other < 2:
-                term = lax.dot_general(
-                    cols[:, row * 3 * deep : (row + 1) * 3 * deep], cot_all[other, :, half],
-                    first, preferred_element_type=F32,
-                )
-                total = term if total is None else total + term
-        rows = pl.ds(ky * 3 * deep, 3 * deep)
-        wg[rows] = total * scale
-        store = pltpu.make_async_copy(wg.at[rows], wgrad_hbm.at[rows], wg_sem.at[ky])
-        store.start()
-        stores.append(store)
+    kept_cot = pltpu.make_async_copy(cot_all.at[:, :, half], half_hbm, out_sem.at[1])
+    kept_cot.start()
 
     second = (((1,), (1,)), ((), ()))
     spread = None
@@ -204,8 +192,44 @@
     out_ref[...] = total.astype(BF16)
     for copy in pending:
         copy.wait_send()
-    for store in stores:
-        store.wait()
+    kept_cols.wait()
+    kept_cot.wait()
+
+
+def filter_kernel(
+    scale, cols_hbm, half_hbm, conv_hbm, igrad_in, out_hbm, igrad_hbm, wgrad_hbm,
+    cols, half, wg, in_sem, through_sem, wg_sem,
+):
+    wide = cols.shape[1] // 2
+    fetch_cols = pltpu.make_async_copy(cols_hbm, cols, in_sem.at[0])
+    fetch_cols.start()
+    fetch_half = pltpu.make_async_copy(half_hbm, half, in_sem.at[1])
+    fetch_half.start()
+    copies = [
+        pltpu.make_async_copy(conv_hbm, out_hbm, through_sem.at[0]),
+        pltpu.make_async_copy(igrad_in, igrad_hbm, through_sem.at[1]),
+    ]
+    for copy in copies:
+        copy.start()
+    fetch_cols.wait()
+    fetch_half.wait()
+    for ky in range(3):
+        total = None
+        for row in range(2):
+            other = row - ky + 1
+            if 0 <= other < 2:
+                term = lax.dot_general(
+                    cols[:, row * wide : (row + 1) * wide], half[other],
+                    (((0,), (0,)), ((), ())), preferred_element_type=F32,
+                )
+                total = term if total is None else total + term
+        rows = pl.ds(ky * wide, wide)
+        wg[rows] = total * scale
+        store = pltpu.make_async_copy(wg.at[rows], wgrad_hbm.at[rows], wg_sem.at[ky])
+        store.start()
+        copies.append(store)
+    for copy in copies:
+        copy.wait()
 
 
 def fused(inputs, weights, cotangent):
@@ -218,14 +242,15 @@
     dma = pltpu.SemaphoreType.DMA
     tile = (breadth, deep)
     outs = pl.pallas_call(
-        functools.partial(fused_kernel, float(total_pixels) ** -0.5),
+        fused_kernel,
         out_shape=[
             jax.ShapeDtypeStruct(tile, BF16),
             jax.ShapeDtypeStruct(tile, BF16),
-            jax.ShapeDtypeStruct((9 * deep, share), F32),
+            jax.ShapeDtypeStruct((breadth, 6 * deep), BF16),
+            jax.ShapeDtypeStruct((2, breadth, share), BF16),
         ],
         in_specs=[hbm, hbm, hbm],
-        out_specs=[vmem, vmem, hbm],
+        out_specs=[vmem, vmem, hbm, hbm],
         scratch_shapes=[
             pltpu.VMEM((9 * deep, channels), BF16),
             pltpu.VMEM((2,) + tile, BF16),
@@ -238,9 +263,8 @@
             pltpu.VMEM((ZS,) + tile, F32),
             pltpu.VMEM((ZS,) + tile, F32),
             pltpu.VMEM((ZS - 1,) + tile, F32),
-            pltpu.VMEM((9 * deep, share), F32),
             dma, dma((2,)), dma((31,)), dma((2, 16)), dma((2 * ZS,)), dma((2 * ZS,)),
-            dma((ZS,)), dma((ZS,)), dma((ZS - 1,)), dma((ZS - 1,)), dma((3,)), dma((3,)), dma((2,)),
+            dma((ZS,)), dma((ZS,)), dma((ZS - 1,)), dma((ZS - 1,)), dma((3,)), dma((2,)), dma((2,)),
         ],
         compiler_params=pltpu.CompilerParams(
             collective_id=0, has_side_effects=True, vmem_limit_bytes=60 * 1024 * 1024
@@ -251,6 +275,23 @@
             transcendentals=0,
         ),
     )(inputs.reshape(tile), cotangent.reshape(tile), weights.reshape(9 * deep, channels))
+    outs = pl.pallas_call(
+        functools.partial(filter_kernel, float(total_pixels) ** -0.5),
+        out_shape=[
+            jax.ShapeDtypeStruct(tile, BF16),
+            jax.ShapeDtypeStruct(tile, BF16),
+            jax.ShapeDtypeStruct((9 * deep, share), F32),
+        ],
+        in_specs=[hbm] * 4,
+        out_specs=[hbm] * 3,
+        scratch_shapes=[
+            pltpu.VMEM((breadth, 6 * deep), BF16),
+            pltpu.VMEM((2, breadth, share), BF16),
+            pltpu.VMEM((9 * deep, share), F32),
+            dma((2,)), dma((2,)), dma((3,)),
+        ],
+        compiler_params=pltpu.CompilerParams(vmem_limit_bytes=60 * 1024 * 1024),
+    )(outs[2], outs[3], outs[0], outs[1])
     return (
         outs[0].reshape(inputs.shape),
         outs[1].reshape(inputs.shape),

time: 42.3 us -> 39.2 us (0.927)
  local copies, waits for them, and re-layouts: 8.19 us -> 0 us
  Pallas kernels: 33.2 us -> 38.4 us
    unnamed x3 -> x0, local copies, waits for them, and re-layouts: 8.19 us -> none
    pallas_call x1 -> x2, Pallas kernels: 33.2 us -> 38.4 us  [the longest x1 33.3 us: fused(): pl.pallas_call(fused_kernel, out_shape=[jax.ShapeDtypeStruct(tile, BF16),...]
where the time goes in v4:
time: 39.2 us; the launch traced here: 39.1 us
  Pallas kernels  38.4 us (98%)
  between operations  0.64 us (2%)
    pallas_call x1, Pallas kernels, fused(): pl.pallas_call(fused_kernel, out_shape=[jax.ShapeDtypeStruct(tile, BF16),...  33.3 us
    pallas_call x1, Pallas kernels, fused(): pl.pallas_call(functools.partial(filter_kernel, float(total_pixels) ** (-...  5.14 us

profile of v4, /device:TPU:0, one launch (start us, length us, event | category | flops | bytes accessed | tf_op | source)
XLA Modules:
  0.0 39.1 jit_solution(8819368418713212037)
XLA Ops:
  0.6 33.3 %shard_map.58 = (bf16[256,128]{1,0:T(8,128)(2,1)}, bf16[256,128]{1,0:T(8,128)(2,1)}, bf16[256,768]{1,0:T(8,128)(2,1)}, bf16[2,256,1024]{2,1,0:T(8,128)(2,1)}) custom-call(bf16[256,128]{1,0:T(8,128)(2,1)} %bitcast.8, bf16[256,128]{1,0:T(8,128)(2,1)} %bitcast.9, bf16[1152,2048]{1,0:T(8,128)(2,1)} %bitcast.6), custom_call_target="tpu_custom_call" | custom-call | flops 3623878656 | bytes 9437184 | tf_op jit(solution)/shard_map/pallas_call | solution.py:244
  33.9 5.1 %shard_map.59 = (bf16[256,128]{1,0:T(8,128)(2,1)}, bf16[256,128]{1,0:T(8,128)(2,1)}, f32[1152,1024]{1,0:T(8,128)}) custom-call(bf16[256,768]{1,0:T(8,128)(2,1)} %get-tuple-element.10.cols_hbm, bf16[2,256,1024]{2,1,0:T(8,128)(2,1)} %get-tuple-element.11.half_hbm, bf16[256,128]{1,0:T(8,128)(2,1)} %get-tuple-element.12.conv_hbm, ...), custom_call_target="tpu_custom_call" | custom-call | tf_op jit(solution)/shard_map/pallas_call | solution.py:278

commit v5 on v4

--- a/solution.py
+++ b/solution.py
@@ -97,7 +97,6 @@
         pass_on(cot_ref, y, chan, z_peers[k - 1])
     pass_on(cot_ref, y, chan, x_peer)
     pass_on(cot_ref, y, chan, y_peer)
-    pass_on(cot_ref, y, chan, sibling)
     own_x.wait()
     own_cot.wait()
 
@@ -117,7 +116,7 @@
     for k in (1, 3, 2):
         ch = chan_of(z_at[k], x, core)
         arrived(y, ch)
-        for to in (x_peer, y_peer, sibling):
+        for to in (x_peer, y_peer):
             pass_on(block(y, ch), y, ch, to)
 
     for load in loads:
@@ -138,14 +137,17 @@
 
     sib_copies = [conv_chunk(i) for i in range(ZS)]
 
-    sib_copies += [conv_chunk(i) for i in range(ZS, 2 * ZS)]
-
     x_copies = []
     for i in range(ZS):
         sib_copies[i].wait_recv()
         x_out[i] = keep[i] + sib_in[i]
         x_copies.append(send(x_out.at[i], x_in.at[i], x_send.at[i], x_recv.at[i], x_peer))
 
+    sib_copies += [conv_chunk(i) for i in range(ZS, 2 * ZS)]
+
+    for k in range(ZS):
+        ch = chan_of(z_at[k], x, core)
+        pass_on(block(y, ch), y, ch, sibling)
     for k in (0, 1, 3, 2):
         ch = chan_of(z_at[k], 1 - x, core)
         arrived(y, ch)
@@ -201,33 +203,50 @@
     cols, half, wg, in_sem, through_sem, wg_sem,
 ):
     wide = cols.shape[1] // 2
-    fetch_cols = pltpu.make_async_copy(cols_hbm, cols, in_sem.at[0])
-    fetch_cols.start()
-    fetch_half = pltpu.make_async_copy(half_hbm, half, in_sem.at[1])
-    fetch_half.start()
+    parts = [pl.ds(row * wide, wide) for row in range(2)]
+    fetches = []
+    for at, (src, dst) in enumerate(
+        [
+            (cols_hbm.at[:, parts[0]], cols.at[:, parts[0]]),
+            (half_hbm.at[1], half.at[1]),
+            (cols_hbm.at[:, parts[1]], cols.at[:, parts[1]]),
+            (half_hbm.at[0], half.at[0]),
+        ]
+    ):
+        fetch = pltpu.make_async_copy(src, dst, in_sem.at[at])
+        fetch.start()
+        fetches.append(fetch)
     copies = [
         pltpu.make_async_copy(conv_hbm, out_hbm, through_sem.at[0]),
         pltpu.make_async_copy(igrad_in, igrad_hbm, through_sem.at[1]),
     ]
     for copy in copies:
         copy.start()
-    fetch_cols.wait()
-    fetch_half.wait()
-    for ky in range(3):
-        total = None
-        for row in range(2):
-            other = row - ky + 1
-            if 0 <= other < 2:
-                term = lax.dot_general(
-                    cols[:, row * wide : (row + 1) * wide], half[other],
-                    (((0,), (0,)), ((), ())), preferred_element_type=F32,
-                )
-                total = term if total is None else total + term
-        rows = pl.ds(ky * wide, wide)
-        wg[rows] = total * scale
-        store = pltpu.make_async_copy(wg.at[rows], wgrad_hbm.at[rows], wg_sem.at[ky])
-        store.start()
-        copies.append(store)
+    fetches[0].wait()
+    fetches[1].wait()
+    piece = wg.shape[1] // 2
+    for ky in (0, 2, 1):
+        if ky == 2:
+            fetches[2].wait()
+            fetches[3].wait()
+        for side in range(2):
+            lanes = pl.ds(side * piece, piece)
+            total = None
+            for row in range(2):
+                other = row - ky + 1
+                if 0 <= other < 2:
+                    term = lax.dot_general(
+                        cols[:, row * wide : (row + 1) * wide], half[other, :, lanes],
+                        (((0,), (0,)), ((), ())), preferred_element_type=F32,
+                    )
+                    total = term if total is None else total + term
+            rows = pl.ds(ky * wide, wide)
+            wg[rows, lanes] = total * scale
+            store = pltpu.make_async_copy(
+                wg.at[rows, lanes], wgrad_hbm.at[rows, lanes], wg_sem.at[2 * ky + side]
+            )
+            store.start()
+            copies.append(store)
     for copy in copies:
         copy.wait()
 
@@ -288,7 +307,7 @@
             pltpu.VMEM((breadth, 6 * deep), BF16),
             pltpu.VMEM((2, breadth, share), BF16),
             pltpu.VMEM((9 * deep, share), F32),
-            dma((2,)), dma((2,)), dma((3,)),
+            dma((4,)), dma((2,)), dma((6,)),
         ],
         compiler_params=pltpu.CompilerParams(vmem_limit_bytes=60 * 1024 * 1024),
     )(outs[2], outs[3], outs[0], outs[1])

time: 39.2 us -> 39.8 us (1.015)
  Pallas kernels: 38.4 us -> 39 us
    pallas_call x1, Pallas kernels: 33.3 us -> 33.8 us  [fused(): pl.pallas_call(fused_kernel, out_shape=[jax.ShapeDtypeStruct(tile, BF16),...]
where the time goes in v5:
time: 39.8 us; the launch traced here: 39.6 us
  Pallas kernels  39 us (98%)
  between operations  0.64 us (2%)
    pallas_call x1, Pallas kernels, fused(): pl.pallas_call(fused_kernel, out_shape=[jax.ShapeDtypeStruct(tile, BF16),...  33.8 us
    pallas_call x1, Pallas kernels, fused(): pl.pallas_call(functools.partial(filter_kernel, float(total_pixels) ** (-...  5.19 us

profile of v5, /device:TPU:0, one launch (start us, length us, event | category | flops | bytes accessed | tf_op | source)
XLA Modules:
  0.0 39.6 jit_solution(18288562318154602870)
XLA Ops:
  0.6 33.8 %shard_map.58 = (bf16[256,128]{1,0:T(8,128)(2,1)}, bf16[256,128]{1,0:T(8,128)(2,1)}, bf16[256,768]{1,0:T(8,128)(2,1)}, bf16[2,256,1024]{2,1,0:T(8,128)(2,1)}) custom-call(bf16[256,128]{1,0:T(8,128)(2,1)} %bitcast.8, bf16[256,128]{1,0:T(8,128)(2,1)} %bitcast.9, bf16[1152,2048]{1,0:T(8,128)(2,1)} %bitcast.6), custom_call_target="tpu_custom_call" | custom-call | flops 3623878656 | bytes 9437184 | tf_op jit(solution)/shard_map/pallas_call | solution.py:263
  34.4 5.2 %shard_map.59 = (bf16[256,128]{1,0:T(8,128)(2,1)}, bf16[256,128]{1,0:T(8,128)(2,1)}, f32[1152,1024]{1,0:T(8,128)}) custom-call(bf16[256,768]{1,0:T(8,128)(2,1)} %get-tuple-element.10.cols_hbm, bf16[2,256,1024]{2,1,0:T(8,128)(2,1)} %get-tuple-element.11.half_hbm, bf16[256,128]{1,0:T(8,128)(2,1)} %get-tuple-element.12.conv_hbm, ...), custom_call_target="tpu_custom_call" | custom-call | tf_op jit(solution)/shard_map/pallas_call | solution.py:297

commit v6 on v4

--- a/solution.py
+++ b/solution.py
@@ -22,7 +22,7 @@
 
 def fused_kernel(
     x_ref, cot_ref, w_hbm, out_ref, igrad_ref, cols_hbm, half_hbm,
-    w_ref, x_all, cols, cot_all, keep, sib_out, sib_in, x_out, x_in, z_out, z_in,
+    w_ref, x_all, cols, cols_t, cot_all, keep, sib_out, sib_in, x_out, x_in, z_out, z_in,
     in_send, in_recv, cot_send, cot_recv, sib_send, sib_recv, x_send, x_recv,
     z_send, z_recv, w_sem, out_sem, own_sem,
 ):
@@ -111,8 +111,6 @@
         cols[:, base : base + deep] = moved(line, 1).astype(BF16)
         cols[:, base + deep : base + 2 * deep] = x_all[row]
         cols[:, base + 2 * deep : base + 3 * deep] = moved(line, -1).astype(BF16)
-    kept_cols = pltpu.make_async_copy(cols, cols_hbm, out_sem.at[0])
-    kept_cols.start()
 
     for k in (1, 3, 2):
         ch = chan_of(z_at[k], x, core)
@@ -151,6 +149,10 @@
         arrived(y, ch)
         for to in (y_peer, sibling):
             pass_on(block(y, ch), y, ch, to)
+
+    cols_t[...] = cols[...].T
+    kept_cols = pltpu.make_async_copy(cols_t, cols_hbm, out_sem.at[0])
+    kept_cols.start()
 
     order = [(k, xx) for xx in (x, 1 - x) for k in (0, 1, 3, 2)]
     z_copies = []
@@ -200,7 +202,7 @@
     scale, cols_hbm, half_hbm, conv_hbm, igrad_in, out_hbm, igrad_hbm, wgrad_hbm,
     cols, half, wg, in_sem, through_sem, wg_sem,
 ):
-    wide = cols.shape[1] // 2
+    wide = cols.shape[0] // 2
     fetch_cols = pltpu.make_async_copy(cols_hbm, cols, in_sem.at[0])
     fetch_cols.start()
     fetch_half = pltpu.make_async_copy(half_hbm, half, in_sem.at[1])
@@ -218,9 +220,9 @@
         for row in range(2):
             other = row - ky + 1
             if 0 <= other < 2:
-                term = lax.dot_general(
-                    cols[:, row * wide : (row + 1) * wide], half[other],
-                    (((0,), (0,)), ((), ())), preferred_element_type=F32,
+                term = jnp.dot(
+                    cols[row * wide : (row + 1) * wide], half[other],
+                    preferred_element_type=F32,
                 )
                 total = term if total is None else total + term
         rows = pl.ds(ky * wide, wide)
@@ -246,7 +248,7 @@
         out_shape=[
             jax.ShapeDtypeStruct(tile, BF16),
             jax.ShapeDtypeStruct(tile, BF16),
-            jax.ShapeDtypeStruct((breadth, 6 * deep), BF16),
+            jax.ShapeDtypeStruct((6 * deep, breadth), BF16),
             jax.ShapeDtypeStruct((2, breadth, share), BF16),
         ],
         in_specs=[hbm, hbm, hbm],
@@ -255,6 +257,7 @@
             pltpu.VMEM((9 * deep, channels), BF16),
             pltpu.VMEM((2,) + tile, BF16),
             pltpu.VMEM((breadth, 6 * deep), BF16),
+            pltpu.VMEM((6 * deep, breadth), BF16),
             pltpu.VMEM((2, breadth, channels), BF16),
             pltpu.VMEM((2 * ZS,) + tile, F32),
             pltpu.VMEM((2 * ZS,) + tile, F32),
@@ -285,7 +288,7 @@
         in_specs=[hbm] * 4,
         out_specs=[hbm] * 3,
         scratch_shapes=[
-            pltpu.VMEM((breadth, 6 * deep), BF16),
+            pltpu.VMEM((6 * deep, breadth), BF16),
             pltpu.VMEM((2, breadth, share), BF16),
             pltpu.VMEM((9 * deep, share), F32),
             dma((2,)), dma((2,)), dma((3,)),

time: 39.2 us -> 39.2 us (level)
  no operation moved by 1% of the time
where the time goes in v6:
time: 39.2 us; the launch traced here: 39.1 us
  Pallas kernels  38.4 us (98%)
  between operations  0.64 us (2%)
    pallas_call x1, Pallas kernels, fused(): pl.pallas_call(fused_kernel, out_shape=[jax.ShapeDtypeStruct(tile, BF16),...  33.3 us
    pallas_call x1, Pallas kernels, fused(): pl.pallas_call(functools.partial(filter_kernel, float(total_pixels) ** (-...  5.14 us

profile of v6, /device:TPU:0, one launch (start us, length us, event | category | flops | bytes accessed | tf_op | source)
XLA Modules:
  0.0 39.1 jit_solution(12160585329264096907)
XLA Ops:
  0.6 33.3 %shard_map.58 = (bf16[256,128]{1,0:T(8,128)(2,1)}, bf16[256,128]{1,0:T(8,128)(2,1)}, bf16[768,256]{1,0:T(8,128)(2,1)}, bf16[2,256,1024]{2,1,0:T(8,128)(2,1)}) custom-call(bf16[256,128]{1,0:T(8,128)(2,1)} %bitcast.8, bf16[256,128]{1,0:T(8,128)(2,1)} %bitcast.9, bf16[1152,2048]{1,0:T(8,128)(2,1)} %bitcast.6), custom_call_target="tpu_custom_call" | custom-call | flops 3623878656 | bytes 9437184 | tf_op jit(solution)/shard_map/pallas_call | solution.py:246
  33.9 5.1 %shard_map.59 = (bf16[256,128]{1,0:T(8,128)(2,1)}, bf16[256,128]{1,0:T(8,128)(2,1)}, f32[1152,1024]{1,0:T(8,128)}) custom-call(bf16[768,256]{1,0:T(8,128)(2,1)} %get-tuple-element.10.cols_hbm, bf16[2,256,1024]{2,1,0:T(8,128)(2,1)} %get-tuple-element.11.half_hbm, bf16[256,128]{1,0:T(8,128)(2,1)} %get-tuple-element.12.conv_hbm, ...), custom_call_target="tpu_custom_call" | custom-call | tf_op jit(solution)/shard_map/pallas_call | solution.py:281
